TPU v7x, 32 devices: a whole 2x2x4 slice. The times are simulated.
32 devices in a mesh: prow: 4 (over z), pcol: 8 (over y, x, core).
Axes of the slice: x: 2, y: 2, z: 4, core: 2. Of those that a mesh axis runs over, the one named last changes fastest.
Arguments:
- left_vecs: bfloat16 [16384, 4096], P(('prow', 'pcol'))
- right_vecs: bfloat16 [16384, 4096], P(('prow', 'pcol'))
- primal: bfloat16 [4096, 4096], P(('prow', 'pcol'))
- dual_inverse: bfloat16 [4096, 4096], P(('prow', 'pcol'))
- owner_map: int32 [32], replicated, may hold values from 0 to 31, each once
- panel_index: int32 [1], replicated, may hold values from 0 to 62
Outputs:
- panel_factor: float32 [256, 16384], P('pcol', 'prow')
- ahead_update: float32 [256, 16384], P('pcol', 'prow')
All inputs are finite; a program needn't handle non-finite values.
Results may differ from a plain program's by a relative error of at most 0.00067.
Values may be sent and summed in bfloat16 or wider, within the bound.
A program may use at most 128 MiB of HBM per device.

v0:
```python
import functools

import jax
import jax.numpy as jnp
from jax import lax
from jax.experimental import pallas as pl
from jax.experimental.pallas import tpu as pltpu
from jax.sharding import PartitionSpec as P

PANEL = 256
BLOCK = 64
HIGH = lax.Precision.HIGHEST
F32 = jnp.float32


def combine(left_prod, right_prod):
    seg = left_prod.shape[1] // 4
    return (
        left_prod[:, seg : 2 * seg] * right_prod[:, 2 * seg : 3 * seg]
        + right_prod[:, seg : 2 * seg] * left_prod[:, 2 * seg : 3 * seg]
        + left_prod[:, 0:seg] * right_prod[:, 3 * seg : 4 * seg]
        + right_prod[:, 0:seg] * left_prod[:, 3 * seg : 4 * seg]
    )


def finish_kernel(grid_rows, grid_cols, block_ref, schur_ref, first_ref, out_ref, work, coef_ref, mixed):
    base = block_ref[:PANEL, :]
    work[:, :PANEL] = 0.5 * (base + base.T)
    rows = lax.broadcasted_iota(jnp.int32, (PANEL, PANEL), 0)
    cols = lax.broadcasted_iota(jnp.int32, (PANEL, PANEL), 1)
    work[:, PANEL:] = jnp.where(rows == cols, 1.0, 0.0).astype(F32)
    row = lax.broadcasted_iota(jnp.int32, (BLOCK, 1), 0)
    brow = lax.broadcasted_iota(jnp.int32, (BLOCK, BLOCK), 0)
    bcol = lax.broadcasted_iota(jnp.int32, (BLOCK, BLOCK), 1)
    eye = jnp.where(brow == bcol, 1.0, 0.0).astype(F32)
    for b in range(PANEL // BLOCK):
        lo = b * BLOCK
        hi = lo + BLOCK
        pair = jnp.concatenate([work[lo:hi, lo:hi], eye], axis=1)
        for k in range(BLOCK):
            pivot = pair[k : k + 1, :]
            scaled = pivot / pair[k : k + 1, k : k + 1]
            factor = jnp.where(row > k, pair[:, k : k + 1], 0.0)
            pair = pair - factor * scaled
        diag = jnp.sum(pair[:, :BLOCK] * eye, axis=1, keepdims=True)
        inv = pair[:, BLOCK:] / jnp.sqrt(diag)
        done = jnp.dot(inv, work[lo:hi, :], precision=HIGH, preferred_element_type=F32)
        work[lo:hi, :] = done
        if hi < PANEL:
            lower = done[:, :PANEL]
            step = lax.dot_general(
                lower, done, (((0,), (0,)), ((), ())), precision=HIGH, preferred_element_type=F32
            )
            work[hi:, :] = work[hi:, :] - step[hi:, :]
    inverse = work[:, PANEL:]
    coef_ref[:PANEL, :] = inverse
    ahead = lax.dot_general(
        block_ref[PANEL:, :],
        inverse,
        (((1,), (1,)), ((), ())),
        precision=HIGH,
        preferred_element_type=F32,
    )
    coef_ref[PANEL:, :] = jnp.dot(ahead, inverse, precision=HIGH, preferred_element_type=F32)
    slots = schur_ref.shape[0]
    height = PANEL // (grid_rows * grid_cols)
    groups = slots // (grid_rows * height)
    narrow = PANEL // grid_cols
    first = first_ref[...]
    ident = lax.broadcasted_iota(jnp.int32, (slots, PANEL), 0)
    both = lax.dot_general(
        schur_ref[:, :PANEL],
        coef_ref[...],
        (((1,), (1,)), ((), ())),
        precision=HIGH,
        preferred_element_type=F32,
    )
    mixed[:, :PANEL] = jnp.where(ident >= first, both[:, :PANEL], 0.0)
    mixed[:, PANEL:] = jnp.where(
        ident >= first + height, schur_ref[:, PANEL:] - both[:, PANEL:], 0.0
    )
    if height % 8:
        out_ref[...] = mixed[...]
        return
    run = 128 // narrow
    for prow in range(grid_rows):
        for half in range(2):
            for group in range(0, groups, run):
                tops = [((group + i) * grid_rows + prow) * height for i in range(run)]
                for pcol in range(grid_cols):
                    lo = half * PANEL + pcol * narrow
                    to = (half * groups + group) * narrow
                    out_ref[prow * grid_cols + pcol, :, to : to + 128] = jnp.concatenate(
                        [mixed[top : top + height, lo : lo + narrow] for top in tops], axis=1
                    )


def finish(panel_block, schur, first_slot, grid_rows, grid_cols):
    devices = grid_rows * grid_cols
    slots = schur.shape[0]
    height = PANEL // devices
    groups = slots // (grid_rows * height)
    narrow = PANEL // grid_cols
    tiled = height % 8 == 0
    shape = (devices, height, 2 * groups * narrow) if tiled else (slots, 2 * PANEL)
    out = pl.pallas_call(
        functools.partial(finish_kernel, grid_rows, grid_cols),
        out_shape=jax.ShapeDtypeStruct(shape, F32),
        in_specs=[pl.BlockSpec(memory_space=pltpu.VMEM)] * 3,
        out_specs=pl.BlockSpec(memory_space=pltpu.VMEM),
        scratch_shapes=[
            pltpu.VMEM((PANEL, 2 * PANEL), F32),
            pltpu.VMEM((2 * PANEL, PANEL), F32),
            pltpu.VMEM((slots, 2 * PANEL), F32),
        ],
        compiler_params=pltpu.CompilerParams(vmem_limit_bytes=24 * 1024 * 1024),
    )(panel_block, schur, jnp.full((1, PANEL), first_slot, jnp.int32))
    if tiled:
        return out
    out = out.reshape(groups, grid_rows, height, 2, grid_cols, narrow)
    return out.transpose(1, 4, 2, 3, 0, 5).reshape(devices, height, 2 * groups * narrow)


def gather_kernel(grid_rows, grid_cols, x_ref, out_ref, local_sem, send_sem, recv_sem):
    prow = lax.axis_index("prow")
    pcol = lax.axis_index("pcol")
    chip = pcol // 2
    core = pcol % 2
    across = grid_cols // 4
    side = chip // across
    place = chip % across

    def column(side_at, place_at, core_at):
        return (side_at * across + place_at) * 2 + core_at

    near = sorted(range(1, grid_rows), key=lambda s: (min(s, grid_rows - s), s))
    along = [(lax.rem(prow + s, grid_rows), pcol) for s in near]
    facing = (prow, column(1 - side, place, core))
    beside = [
        (prow, column(side, lax.rem(place + t, across), core)) for t in range(1, across)
    ]
    sibling = (prow, column(side, place, 1 - core))
    barrier = pltpu.get_barrier_semaphore()
    peers = along + [facing] + beside + [sibling]
    for peer in peers:
        pl.semaphore_signal(barrier, inc=1, device_id=peer, device_id_type=pl.DeviceIdType.MESH)
    pl.semaphore_wait(barrier, len(peers))

    sends = []

    def send(src, slot, peer):
        copy = pltpu.make_async_remote_copy(
            src_ref=src,
            dst_ref=out_ref.at[slot],
            send_sem=send_sem.at[len(sends)],
            recv_sem=recv_sem.at[slot],
            device_id=peer,
            device_id_type=pl.DeviceIdType.MESH,
        )
        copy.start()
        sends.append(copy)

    def arrive(slot):
        pltpu.make_async_remote_copy(
            src_ref=out_ref.at[slot],
            dst_ref=out_ref.at[slot],
            send_sem=send_sem.at[0],
            recv_sem=recv_sem.at[slot],
            device_id=sibling,
            device_id_type=pl.DeviceIdType.MESH,
        ).wait_recv()

    def slot_of(row, col, half):
        return (row * grid_cols + col) * 2 + half

    def pass_on(slot, to):
        arrive(slot)
        for peer in to:
            send(out_ref.at[slot], slot, peer)

    mine = slot_of(prow, pcol, 0)
    local = pltpu.make_async_copy(x_ref, out_ref.at[pl.ds(mine, 2)], local_sem)
    local.start()
    for half in range(2):
        for peer in [facing] + beside + along + [sibling]:
            send(x_ref.at[half], mine + half, peer)

    def from_plane(row):
        for half in range(2):
            slot = slot_of(row, facing[1], half)
            pass_on(slot, (beside if half == 0 else []) + [sibling])
            for peer in beside:
                slot = slot_of(row, peer[1], half)
                pass_on(slot, ([facing] if half == 1 else []) + [sibling])

    def from_corner(row):
        for t in range(1, across):
            col = column(1 - side, lax.rem(place + t, across), core)
            for half in range(2):
                pass_on(slot_of(row, col, half), [sibling])

    rows = [prow] + [peer[0] for peer in along]
    for step in range(grid_rows + 2):
        if 0 < step < grid_rows:
            for half in range(2):
                pass_on(slot_of(rows[step], pcol, half), [facing] + beside + [sibling])
        if 1 <= step <= grid_rows:
            from_plane(rows[step - 1])
        if 2 <= step:
            from_corner(rows[step - 2])
    for row in rows:
        for side_at in (side, 1 - side):
            for t in range(across):
                col = column(side_at, lax.rem(place + t, across), 1 - core)
                for half in range(2):
                    arrive(slot_of(row, col, half))
    local.wait()
    for copy in sends:
        copy.wait_send()


def gather(x, collective_id, tile):
    grid_rows = lax.axis_size("prow")
    grid_cols = lax.axis_size("pcol")
    devices = grid_rows * grid_cols
    rows, columns = x.shape
    if grid_cols % 4 or rows % (2 * tile):
        return lax.all_gather(x, ("prow", "pcol"), axis=0, tiled=True)
    across = grid_cols // 4
    count = 2 * (grid_rows - 1 + grid_rows * across + grid_rows * grid_cols // 2)
    count += 2 * grid_rows * (across - 1)
    out = pl.pallas_call(
        functools.partial(gather_kernel, grid_rows, grid_cols),
        out_shape=jax.ShapeDtypeStruct((2 * devices, rows // 2, columns), x.dtype),
        in_specs=[pl.BlockSpec(memory_space=pl.ANY)],
        out_specs=pl.BlockSpec(memory_space=pl.ANY),
        scratch_shapes=[
            pltpu.SemaphoreType.DMA,
            pltpu.SemaphoreType.DMA((count,)),
            pltpu.SemaphoreType.DMA((2 * devices,)),
        ],
        compiler_params=pltpu.CompilerParams(
            collective_id=collective_id, has_side_effects=True
        ),
    )(x.reshape(2, rows // 2, columns))
    return out.reshape(devices * rows, columns)


def body(left_vecs, right_vecs, primal, dual_inverse, owner_map, panel_index):
    devices = lax.axis_size(("prow", "pcol"))
    grid_rows = lax.axis_size("prow")
    grid_cols = lax.axis_size("pcol")
    height = PANEL // devices
    slots = left_vecs.shape[0]
    order = left_vecs.shape[1]
    feats = primal.shape[0]
    start = panel_index[0] * PANEL
    first_slot = start // devices
    wide = lax.broadcasted_iota(jnp.int32, (devices, height, height, devices), 0)
    perm = (wide == owner_map[None, None, None, :]) & (
        lax.broadcasted_iota(jnp.int32, wide.shape, 1)
        == lax.broadcasted_iota(jnp.int32, wide.shape, 2)
    )
    perm = perm.astype(jnp.bfloat16).reshape(PANEL, PANEL)
    perm32 = perm.astype(F32)

    panel_left = lax.dynamic_slice_in_dim(left_vecs, first_slot, 2 * height, 0)
    panel_right = lax.dynamic_slice_in_dim(right_vecs, first_slot, 2 * height, 0)
    own_vecs = jnp.concatenate([panel_left, panel_right], axis=0)
    panel_vecs = gather(own_vecs, 0, 16)
    matrices = jnp.concatenate([primal, dual_inverse], axis=0)
    raw = lax.dot_general(
        panel_vecs, matrices, (((1,), (1,)), ((), ())), preferred_element_type=F32
    )
    raw = raw.reshape(devices, 4, height, 2 * feats).transpose(1, 0, 2, 3)
    raw = raw.reshape(4, PANEL, 2, feats).astype(jnp.bfloat16)
    images = jnp.einsum("vkgf,kj->fgvj", raw, perm, preferred_element_type=F32)
    images = images.astype(jnp.bfloat16).reshape(feats, 8 * PANEL)
    piece = gather(images, 1, 16)
    early = jnp.dot(own_vecs, piece, preferred_element_type=F32)
    own_panel = combine(early[: 2 * height], early[2 * height :])
    panel_rows = lax.all_gather(own_panel, ("prow", "pcol"), axis=0, tiled=True)
    left_prod = jnp.dot(left_vecs, piece, preferred_element_type=F32)
    right_prod = jnp.dot(right_vecs, piece, preferred_element_type=F32)
    schur = combine(left_prod, right_prod)

    panel_rows = panel_rows[:, :PANEL]
    panel_rows = panel_rows.reshape(devices, 2, height, PANEL).transpose(1, 0, 2, 3)
    panel_block = jnp.einsum(
        "kj,pkc->pjc",
        perm32,
        panel_rows.reshape(2, PANEL, PANEL),
        precision=HIGH,
        preferred_element_type=F32,
    ).reshape(2 * PANEL, PANEL)
    groups = slots // (grid_rows * height)
    narrow = PANEL // grid_cols
    outgoing = finish(panel_block, schur, first_slot, grid_rows, grid_cols)
    arrived = lax.all_to_all(outgoing, ("prow", "pcol"), split_axis=0, concat_axis=0, tiled=True)
    final = lax.dot_general(
        arrived.reshape(PANEL, groups * 2 * narrow),
        perm32,
        (((0,), (0,)), ((), ())),
        precision=HIGH,
        preferred_element_type=F32,
    )
    final = final.reshape(2, groups, narrow, PANEL).transpose(0, 2, 1, 3)
    final = final.reshape(2, narrow, groups * PANEL)
    return (final[0], final[1])


def solution(mesh):
    return jax.shard_map(
        body,
        mesh=mesh,
        in_specs=(
            P(("prow", "pcol"), None),
            P(("prow", "pcol"), None),
            P(("prow", "pcol"), None),
            P(("prow", "pcol"), None),
            P(),
            P(),
        ),
        out_specs=(P("pcol", "prow"), P("pcol", "prow")),
        check_vma=False,
    )
```

profile of v0, /device:TPU:0, one launch (start us, length us, event | category | flops | bytes accessed | tf_op | source)
XLA Modules:
  0.0 302.1 jit_solution(9425055472008510559)
XLA Ops:
  7.2 0.0 all-gather.2.cloned.1.call-start
  7.9 1.1 constant_dynamic-slice_fusion
  9.0 0.7 pad_maximum_fusion
  9.7 46.8 %shard_map.77 = bf16[64,16,4096]{2,1,0:T(8,128)(2,1)} custom-call(bf16[2,16,4096]{2,1,0:T(8,128)(2,1)} %bitcast.74), custom_call_target="tpu_custom_call" | custom-call | tf_op jit(solution)/shard_map/pallas_call | solution.py:232
  56.5 0.0 copy-start.1
  56.5 5.8 %fusion.5 = bf16[4,32,8,256]{3,2,0,1:T(8,128)(2,1)S(1)} fusion(bf16[32,4,8,4096]{3,2,1,0:T(8,128)(2,1)} %bitcast.68, bf16[128,4096]{1,0:T(8,128)(2,1)S(1)} %copy-done.2, bf16[128,4096]{1,0:T(8,128)(2,1)S(1)} %copy-done.3), kind=kOutput, calls=%fused_computation.10 | convolution fusion | flops 2151940096 | bytes 11010048 | tf_op jit(solution)/shard_map/dot_general | solution.py:272
  62.3 0.1 convert_element_type.19
  62.5 0.1 iota.40
  62.6 0.1 eq.18
  62.7 0.1 iota.37
  62.8 0.1 iota.34
  62.8 0.5 fusion.4
  63.3 0.4 copy.18
  63.7 1.2 reshape_reshape.3.x_ref
  64.9 86.5 %shard_map.78 = bf16[64,64,2048]{2,1,0:T(8,128)(2,1)} custom-call(bf16[2,64,2048]{2,1,0:T(8,128)(2,1)} %reshape_reshape.3.x_ref), custom_call_target="tpu_custom_call" | custom-call | tf_op jit(solution)/shard_map/pallas_call | solution.py:232
  151.4 8.7 %fusion.32 = f32[32,2048]{1,0:T(8,128)S(1)} fusion(bf16[4096,2048]{1,0:T(8,128)(2,1)} %bitcast.65, bf16[16,4096]{1,0:T(8,128)(2,1)S(1)} %get-tuple-element.4, bf16[16,4096]{1,0:T(8,128)(2,1)S(1)} %get-tuple-element.5), kind=kOutput, calls=%fused_computation.49 | convolution fusion | flops 537395200 | bytes 17301504 | tf_op jit(solution)/shard_map/dot_general | solution.py:280
  160.1 0.6 fusion.28
  160.8 0.0 all-gather.2.cloned.1.call-update
  160.8 13.8 %convolution_bitcast_fusion.1 = f32[512,2048]{1,0:T(8,128)S(1)} fusion(bf16[512,4096]{1,0:T(8,128)(2,1)} %param.6, bf16[4096,2048]{1,0:T(8,128)(2,1)} %bitcast.66), kind=kOutput, calls=%fused_computation.1 | convolution fusion | flops 8589934592 | bytes 25165824 | tf_op jit(solution)/shard_map/dot_general | solution.py:283
  174.6 0.0 copy-done
  174.6 11.1 %convolution_bitcast_fusion = f32[512,2048]{1,0:T(8,128)S(1)} fusion(bf16[512,4096]{1,0:T(8,128)(2,1)} %param.7, bf16[4096,2048]{1,0:T(8,128)(2,1)S(1)} %bitcast.67), kind=kOutput, calls=%fused_computation | convolution fusion | flops 8589934592 | bytes 25165824 | tf_op jit(solution)/shard_map/dot_general | solution.py:284
  185.7 1.0 fusion.6.schur_ref
  186.7 47.2 %all-gather.2.cloned.1.call-done = f32[512,512]{1,0:T(8,128)} async-done(((f32[16,512]{1,0:T(8,128)}), f32[512,512]{1,0:T(8,128)}) %all-gather.2.cloned.1.call-update) | async-done | bytes 1048592 | tf_op jit(solution)/shard_map/all_gather | solution.py:282
  233.9 1.1 slice.96
  235.0 0.6 fusion.9
  235.6 27.2 %shard_map.79 = f32[32,8,1024]{2,1,0:T(8,128)S(1)} custom-call(f32[512,256]{1,0:T(8,128)S(1)} %bitcast.64, f32[512,512]{1,0:T(8,128)S(1)} %fusion.6.schur_ref, s32[1,256]{1,0:T(1,128)S(1)} %broadcast_in_dim.4.first_ref), custom_call_target="tpu_custom_call" | custom-call | tf_op jit(solution)/shard_map/pallas_call | solution.py:106
  262.8 29.6 %all_to_all.5 = f32[32,8,1024]{2,1,0:T(8,128)S(1)} all-to-all(f32[32,8,1024]{2,1,0:T(8,128)S(1)} %shard_map.79), channel_id=1, replica_groups=mesh['prow'=4,'pcol'=8] {'prow','pcol'}, dimensions={0} | all-to-all | bytes 2097152 | tf_op jit(solution)/shard_map/all_to_all | solution.py:299
  292.4 0.3 copy.23
  292.7 0.7 convolution_bitcast_fusion.2
  293.5 0.1 fusion.33
  293.6 0.8 copy.34
  294.4 0.8 copy.35
  (12 shorter events, 0.1 us)
Async XLA Ops:
  7.2 226.8 %all-gather.2.cloned.1.call-start = ((), (), s32[]{:S(2)}) async-start(), calls=%async_computation.1 | async-start | bytes 1081344 | tf_op jit(solution)/shard_map/all_gather | solution.py:282
  9.7 46.8 %copy-start.2 = (bf16[128,4096]{1,0:T(8,128)(2,1)S(1)}, bf16[128,4096]{1,0:T(8,128)(2,1)}, u32[]{:S(2)}) copy-start(bf16[128,4096]{1,0:T(8,128)(2,1)} %param.9) | copy-start | bytes 3145732
  9.7 46.8 %copy-start.3 = (bf16[128,4096]{1,0:T(8,128)(2,1)S(1)}, bf16[128,4096]{1,0:T(8,128)(2,1)}, u32[]{:S(2)}) copy-start(bf16[128,4096]{1,0:T(8,128)(2,1)} %param.8) | copy-start | bytes 3145732
  56.5 6.0 %copy-start.1 = (s32[32]{0:T(128)S(1)}, s32[32]{0:T(128)}, u32[]{:S(2)}) copy-start(s32[32]{0:T(128)} %param.10) | copy-start | bytes 388
  160.8 13.8 %copy-start = (bf16[64,64,2048]{2,1,0:T(8,128)(2,1)S(1)}, bf16[64,64,2048]{2,1,0:T(8,128)(2,1)}, u32[]{:S(2)}) copy-start(bf16[64,64,2048]{2,1,0:T(8,128)(2,1)} %shard_map.78) | copy-start | bytes 50331652
Sparse Core Ops, SparseCore 0:
  160.9 72.9 all-gather.1
where the time goes:
time: 302 us
  Pallas kernels  160 us (53%)
  waiting for transfers between devices  47.3 us (16%)
  matrix products  41 us (14%)
  blocking collectives  29.6 us (10%)
  between operations  14.9 us (5%)
  local copies, waits for them, and re-layouts  6.42 us (2%)
    pallas_call x2, Pallas kernels, gather(): pl.pallas_call(functools.partial(gather_kernel, grid_rows, grid_cols), ou...  133 us
    all_gather x1, waiting for transfers between devices, body(): panel_rows = lax.all_gather(own_panel, ('prow', 'pcol'), axis=0, tiled=True)  47.2 us
    all_to_all x1, blocking collectives, body(): lax.all_to_all(outgoing, ('prow', 'pcol'), split_axis=0, concat_axis=0, t...  29.6 us
    pallas_call x1, Pallas kernels, finish(): pl.pallas_call(functools.partial(finish_kernel, grid_rows, grid_cols), ou...  27.2 us
    dot_general x1, matrix products, body(): left_prod = jnp.dot(left_vecs, piece, preferred_element_type=F32)  13.8 us
    dot_general x1, matrix products, body(): right_prod = jnp.dot(right_vecs, piece, preferred_element_type=F32)  11.1 us
    dot_general x1, matrix products, body(): early = jnp.dot(own_vecs, piece, preferred_element_type=F32)  8.75 us
  transfers between devices with their start and end apart: 1, of which 1 were waited for; matrix products, arithmetic and copies ran while one was open for 9% of the time, Pallas kernels for 0%

commit v1 on v0

--- a/solution.py
+++ b/solution.py
@@ -277,14 +277,12 @@
     images = jnp.einsum("vkgf,kj->fgvj", raw, perm, preferred_element_type=F32)
     images = images.astype(jnp.bfloat16).reshape(feats, 8 * PANEL)
     piece = gather(images, 1, 16)
-    early = jnp.dot(own_vecs, piece, preferred_element_type=F32)
-    own_panel = combine(early[: 2 * height], early[2 * height :])
-    panel_rows = lax.all_gather(own_panel, ("prow", "pcol"), axis=0, tiled=True)
     left_prod = jnp.dot(left_vecs, piece, preferred_element_type=F32)
     right_prod = jnp.dot(right_vecs, piece, preferred_element_type=F32)
     schur = combine(left_prod, right_prod)
 
-    panel_rows = panel_rows[:, :PANEL]
+    own_panel = lax.dynamic_slice_in_dim(schur[:, :PANEL], first_slot, 2 * height, 0)
+    panel_rows = gather(own_panel, 2, 8)
     panel_rows = panel_rows.reshape(devices, 2, height, PANEL).transpose(1, 0, 2, 3)
     panel_block = jnp.einsum(
         "kj,pkc->pjc",

time: 302 us -> 271 us (0.90)
  waiting for transfers between devices: 47.3 us -> 0 us
  Pallas kernels: 160 us -> 198 us
  between operations: 14.9 us -> 1.52 us
  matrix products: 41 us -> 33.4 us
    all_gather x1 -> x0, waiting for transfers between devices: 47.2 us -> none  [body(): panel_rows = lax.all_gather(own_panel, ('prow', 'pcol'), axis=0, tiled=True)]
    pallas_call x2 -> x3, Pallas kernels: 133 us -> 171 us  [gather(): pl.pallas_call(functools.partial(gather_kernel, grid_rows, grid_cols), ou...]
    dot_general x1 -> x0, matrix products: 8.75 us -> none  [body(): early = jnp.dot(own_vecs, piece, preferred_element_type=F32)]
  transfers between devices with their start and end apart: 1 -> 0, of which waited for: 1 -> 0; matrix products, arithmetic and copies ran while one was open for 9% -> 0% of each run, Pallas kernels for 0% -> 0%
where the time goes in v1:
time: 271 us
  Pallas kernels  198 us (73%)
  matrix products  33.4 us (12%)
  blocking collectives  30.2 us (11%)
  local copies, waits for them, and re-layouts  6 us (2%)
    pallas_call x3, Pallas kernels, gather(): pl.pallas_call(functools.partial(gather_kernel, grid_rows, grid_cols), ou...  171 us
    all_to_all x1, blocking collectives, body(): lax.all_to_all(outgoing, ('prow', 'pcol'), split_axis=0, concat_axis=0, t...  30.2 us
    pallas_call x1, Pallas kernels, finish(): pl.pallas_call(functools.partial(finish_kernel, grid_rows, grid_cols), ou...  27.2 us
    dot_general x1, matrix products, body(): right_prod = jnp.dot(right_vecs, piece, preferred_element_type=F32)  13.6 us
    dot_general x1, matrix products, body(): left_prod = jnp.dot(left_vecs, piece, preferred_element_type=F32)  11.2 us
    dot_general x1, matrix products, body(): lax.dot_general(panel_vecs, matrices, (((1,), (1,)), ((), ())), preferred...  5.85 us

profile of v1, /device:TPU:0, one launch (start us, length us, event | category | flops | bytes accessed | tf_op | source)
XLA Modules:
  0.0 270.6 jit_solution(12505628260728778465)
XLA Ops:
  1.3 1.1 constant_dynamic-slice_fusion
  2.4 0.7 pad_maximum_fusion
  3.1 46.8 %shard_map.77 = bf16[64,16,4096]{2,1,0:T(8,128)(2,1)} custom-call(bf16[2,16,4096]{2,1,0:T(8,128)(2,1)} %bitcast.74), custom_call_target="tpu_custom_call" | custom-call | tf_op jit(solution)/shard_map/pallas_call | solution.py:232
  49.9 0.0 copy-done.2
  49.9 0.0 copy-done.3
  50.0 0.0 copy-start.1
  50.0 5.9 %fusion.5 = bf16[4,32,8,256]{3,2,0,1:T(8,128)(2,1)S(1)} fusion(bf16[32,4,8,4096]{3,2,1,0:T(8,128)(2,1)} %bitcast.68, bf16[128,4096]{1,0:T(8,128)(2,1)S(1)} %copy-done.2, bf16[128,4096]{1,0:T(8,128)(2,1)S(1)} %copy-done.3), kind=kOutput, calls=%fused_computation.10 | convolution fusion | flops 2151940096 | bytes 11010048 | tf_op jit(solution)/shard_map/dot_general | solution.py:272
  55.9 0.1 convert_element_type.19
  56.0 0.1 iota.34
  56.1 0.1 iota.37
  56.2 0.0 copy-done.1
  56.2 0.1 eq.18
  56.3 0.1 iota.40
  56.4 0.5 fusion.4
  56.8 0.4 copy.16
  57.3 1.2 reshape_reshape.6.x_ref
  58.4 86.5 %shard_map.78 = bf16[64,64,2048]{2,1,0:T(8,128)(2,1)} custom-call(bf16[2,64,2048]{2,1,0:T(8,128)(2,1)} %reshape_reshape.6.x_ref), custom_call_target="tpu_custom_call" | custom-call | tf_op jit(solution)/shard_map/pallas_call | solution.py:232
  144.9 0.0 copy-start
  144.9 13.6 %convolution_bitcast_fusion = f32[512,2048]{1,0:T(8,128)S(1)} fusion(bf16[512,4096]{1,0:T(8,128)(2,1)} %param.7, bf16[4096,2048]{1,0:T(8,128)(2,1)} %bitcast.66), kind=kOutput, calls=%fused_computation | convolution fusion | flops 8589934592 | bytes 25165824 | tf_op jit(solution)/shard_map/dot_general | solution.py:281
  158.5 0.0 copy-done
  158.5 11.2 %convolution_bitcast_fusion.1 = f32[512,2048]{1,0:T(8,128)S(1)} fusion(bf16[512,4096]{1,0:T(8,128)(2,1)} %param.6, bf16[4096,2048]{1,0:T(8,128)(2,1)S(1)} %bitcast.67), kind=kOutput, calls=%fused_computation.1 | convolution fusion | flops 8589934592 | bytes 25165824 | tf_op jit(solution)/shard_map/dot_general | solution.py:280
  169.7 1.0 fusion.6.schur_ref
  170.8 0.6 dynamic-slice_bitcast_fusion.x_ref
  171.4 37.3 %shard_map.79 = f32[64,8,256]{2,1,0:T(8,128)} custom-call(f32[2,8,256]{2,1,0:T(8,128)} %dynamic-slice_bitcast_fusion.x_ref), custom_call_target="tpu_custom_call" | custom-call | tf_op jit(solution)/shard_map/pallas_call | solution.py:232
  208.8 1.6 fusion.9
  210.4 27.2 %shard_map.80 = f32[32,8,1024]{2,1,0:T(8,128)S(1)} custom-call(f32[512,256]{1,0:T(8,128)S(1)} %bitcast.65, f32[512,512]{1,0:T(8,128)S(1)} %fusion.6.schur_ref, s32[1,256]{1,0:T(1,128)S(1)} %broadcast_in_dim.4.first_ref), custom_call_target="tpu_custom_call" | custom-call | tf_op jit(solution)/shard_map/pallas_call | solution.py:106
  237.6 30.2 %all_to_all.5 = f32[32,8,1024]{2,1,0:T(8,128)S(1)} all-to-all(f32[32,8,1024]{2,1,0:T(8,128)S(1)} %shard_map.80), channel_id=1, replica_groups=mesh['prow'=4,'pcol'=8] {'prow','pcol'}, dimensions={0} | all-to-all | bytes 2097152 | tf_op jit(solution)/shard_map/all_to_all | solution.py:297
  267.8 0.3 copy.19
  268.1 0.7 convolution_bitcast_fusion.2
  268.8 0.1 fusion.29
  269.0 0.8 copy.28
  269.8 0.8 copy.29
  (9 shorter events, 0.1 us)
Async XLA Ops:
  3.1 46.8 %copy-start.2 = (bf16[128,4096]{1,0:T(8,128)(2,1)S(1)}, bf16[128,4096]{1,0:T(8,128)(2,1)}, u32[]{:S(2)}) copy-start(bf16[128,4096]{1,0:T(8,128)(2,1)} %param.9) | copy-start | bytes 3145732
  3.1 46.8 %copy-start.3 = (bf16[128,4096]{1,0:T(8,128)(2,1)S(1)}, bf16[128,4096]{1,0:T(8,128)(2,1)}, u32[]{:S(2)}) copy-start(bf16[128,4096]{1,0:T(8,128)(2,1)} %param.8) | copy-start | bytes 3145732
  50.0 6.2 %copy-start.1 = (s32[32]{0:T(128)S(1)}, s32[32]{0:T(128)}, u32[]{:S(2)}) copy-start(s32[32]{0:T(128)} %param.10) | copy-start | bytes 388
  144.9 13.6 %copy-start = (bf16[64,64,2048]{2,1,0:T(8,128)(2,1)S(1)}, bf16[64,64,2048]{2,1,0:T(8,128)(2,1)}, u32[]{:S(2)}) copy-start(bf16[64,64,2048]{2,1,0:T(8,128)(2,1)} %shard_map.78) | copy-start | bytes 50331652
